TPU v7x, 256 devices: a whole 4x4x8 slice. The times are simulated.
256 devices in a mesh: tm: 16 (over x_hi, y, core), rows: 16 (over x_lo, z).
Axes of the slice: x: 4 (x_hi: 2, x_lo: 2; x = x_hi * 2 + x_lo), y: 4, z: 8, core: 2. Of those that a mesh axis runs over, the one named last changes fastest.
Arguments:
- snapshots: bfloat16 [32768, 32768], P('tm', 'rows'), may hold values from -6 to 6
- spod_modes: bfloat16 [64, 2, 4, 32768], P('tm', None, None, 'rows'), may hold values from -0.046875 to 0.046875
- freq_index: int32 [64], replicated, may hold values from 1 to 128, as said below
- seg_offsets: int32 [8192], P('tm'), may hold values from 0 to 2047, as said below
Outputs:
- coefficients: float32 [64, 2, 4, 8192], P('rows', None, None, 'tm')
Inputs may be any that keep to these rules, and one draw needn't show every extreme that they name: Frequency f is bin freq_index[f] of a segment of 256 snapshots; values may repeat. Segment n starts at snapshot (n // 512) * 2048 + seg_offsets[n]; snapshots past the last one count as zeros.
All inputs are finite; a program needn't handle non-finite values.
Results may differ from a plain program's by a relative error of at most 0.0003.
Values may be sent and summed in bfloat16 or wider, within the bound.
A program may use at most 64 MiB of HBM per device.

v0:
```python
import math

import jax
import jax.numpy as jnp
from jax import lax
from jax.sharding import PartitionSpec as P

F = 64
M = 4
L = 256


def from_behind(block, axis, distance):
    devices = range(lax.axis_size(axis))
    route = [(i - distance, i) for i in devices if i - distance in devices]
    return lax.ppermute(block, axis, route)


def hann_weights(distance):
    inside = (distance >= 0) & (distance < L)
    angles = distance.astype(jnp.float32) * (2.0 * math.pi / L)
    values = math.sqrt(8.0 / (3.0 * L)) * (0.5 - 0.5 * jnp.cos(angles))
    return jnp.where(inside, values, 0.0)


def phase_pair(frequency, moments):
    phase_bin = frequency[:, None] * moments[None, :] % L
    angles = phase_bin.astype(jnp.float32) * (2.0 * math.pi / L)
    return (jnp.cos(angles)[:, None, :], jnp.sin(angles)[:, None, :])


def demodulate(projected, frequency, moments):
    cosine, sine_part = phase_pair(frequency, moments)
    real_in = projected[:, 0]
    imag_in = projected[:, 1]
    real_out = cosine * real_in - sine_part * imag_in
    imag_out = -(sine_part * real_in + cosine * imag_in)
    return jnp.stack([real_out, imag_out], 1)


def envelope(extended, offsets, frequency, base_time):
    distance = jnp.arange(extended.shape[3], dtype=jnp.int32)[None, :] - offsets[:, None]
    weights = hann_weights(distance)
    groups = extended.shape[0]
    flat_rows = extended.reshape(groups * extended.shape[1] * extended.shape[2], extended.shape[3])
    summed = lax.dot_general(
        flat_rows,
        weights,
        (((1,), (1,)), ((), ())),
        precision=lax.Precision.HIGHEST,
        preferred_element_type=jnp.float32,
    )
    summed = summed.reshape(groups, 2, extended.shape[2], offsets.shape[0])
    cosine, sine_part = phase_pair(frequency, base_time + offsets)
    env_real = summed[:, 0]
    env_imag = summed[:, 1]
    return jnp.stack(
        [cosine * env_real - sine_part * env_imag, sine_part * env_real + cosine * env_imag], 1
    )


def body(snapshots, spod_modes, freq_index, seg_offsets):
    time_len = snapshots.shape[0]
    tm_pos = lax.axis_index("tm")
    row_pos = lax.axis_index("rows")
    block_rows = lax.all_gather(spod_modes, "tm", axis=0, tiled=True)
    groups = block_rows.shape[0]
    flat_modes = block_rows.reshape(groups * 2 * M, block_rows.shape[3])
    partial_sums = lax.dot_general(
        flat_modes, snapshots, (((1,), (1,)), ((), ())), preferred_element_type=jnp.float32
    )
    projected = partial_sums.reshape(groups, 2, M, snapshots.shape[0])
    share_len = F // lax.axis_size("rows")
    own_freqs = lax.dynamic_slice_in_dim(freq_index, row_pos * share_len, share_len, 0)
    moments = tm_pos * time_len + jnp.arange(snapshots.shape[0], dtype=jnp.int32)
    base_time = tm_pos * time_len
    summed = lax.psum(projected, "rows")
    own_share = lax.dynamic_slice_in_dim(summed, row_pos * share_len, share_len, 0)
    demodulated = demodulate(own_share, own_freqs, moments)
    next_part = from_behind(demodulated[:, :, :, :L], "tm", -1)
    extended = jnp.concatenate([demodulated, next_part], 3)
    return envelope(extended, seg_offsets, own_freqs, base_time)


def solution(mesh):
    placed = (P("tm", "rows"), P("tm", None, None, "rows"), P(), P("tm"))
    return jax.shard_map(
        body, mesh=mesh, in_specs=placed, out_specs=P("rows", None, None, "tm"), check_vma=False
    )
```

profile of v0, /device:TPU:27, one launch (start us, length us, event | category | flops | bytes accessed | tf_op | source)
XLA Modules:
  0.0 264.1 jit_solution(10971846366620990321)
XLA Ops:
  6.5 0.0 all-gather.2.cloned.1.call-start
  6.5 0.7 all-gather.2.cloned.1.call-update
  7.3 0.0 copy-start.1
  7.3 0.0 copy-start
  7.3 0.0 all-reduce.2.cloned.1.call-start
  7.3 57.3 %all-gather.2.cloned.1.call-done = bf16[64,2,4,2048]{3,2,1,0:T(4,128)(2,1)} async-done(((bf16[4,2,4,2048]{3,2,1,0:T(4,128)(2,1)}), bf16[64,2,4,2048]{3,2,1,0:T(4,128)(2,1)}) %all-gather.2.cloned.1.call-update) | async-done | bytes 2097168 | tf_op jit(solution)/shard_map/all_gather | solution.py:66
  64.6 11.0 %fusion = f32[64,2,4,2048]{3,0,2,1:T(8,128)} fusion(bf16[2048,2048]{1,0:T(8,128)(2,1)} %param.4, bf16[64,2,4,2048]{3,2,1,0:T(4,128)(2,1)} %all-gather.2.cloned.1.call-done), kind=kOutput, calls=%fused_computation | convolution fusion | flops 4294967296 | bytes 14680064 | tf_op jit(solution)/shard_map/dot_general | solution.py:69
  75.6 0.0 all-reduce.2.cloned.1.call-update
  75.7 0.0 copy-done.1
  75.7 0.1 dynamic_slice.6
  75.7 0.0 copy-done
  75.8 0.3 fusion.32
  76.1 143.5 %all-reduce.2.cloned.1.call-done = f32[64,2,4,2048]{3,0,2,1:T(8,128)} async-done(((f32[64,2,4,2048]{3,0,2,1:T(8,128)}), f32[64,2,4,2048]{3,0,2,1:T(8,128)}) %all-reduce.2.cloned.1.call-update) | async-done | bytes 4194320 | tf_op jit(solution)/shard_map/psum | solution.py:77
  219.6 1.1 multiply_subtract_fusion
  220.8 11.2 %collective-permute-start = (f32[4,2,4,256]{3,0,2,1:T(4,128)S(1)}, f32[4,2,4,256]{3,0,2,1:T(4,128)S(1)}, u32[]{:S(2)}, u32[]{:S(2)}) collective-permute-start(f32[4,2,4,256]{3,0,2,1:T(4,128)S(1)} %pad_maximum_fusion.1), channel_id=1, source_target_pairs={{16,0},{32,16},{48,32},{64,48},{80,64},{96,80},{112,96},{128,112},... | collective-permute-start | bytes 98312 | tf_op jit(solution)/shard_map/ppermute | solution.py:16
  231.9 0.2 fusion.37
  232.1 3.8 %collective-permute-done = f32[4,2,4,256]{3,0,2,1:T(4,128)S(1)} collective-permute-done((f32[4,2,4,256]{3,0,2,1:T(4,128)S(1)}, f32[4,2,4,256]{3,0,2,1:T(4,128)S(1)}, u32[]{:S(2)}, u32[]{:S(2)}) %collective-permute-start) | collective-permute-done | bytes 32800 | tf_op jit(solution)/shard_map/ppermute | solution.py:16
  235.9 20.7 %fusion.2 = f32[4,2,4,512]{3,0,2,1:T(4,128)S(1)} fusion(s32[512]{0:T(512)S(1)} %copy-done, f32[4,2,4,256]{3,0,2,1:T(4,128)S(1)} %collective-permute-done, f32[4,1,4,2048]{3,0,2,1:T(4,128)S(1)} %get-tuple-element.6, f32[4,1,4,2048]{3,0,2,1:T(4,128)S(1)} %get-tuple-element.5), kind=kOutput, calls=%fused_computation.2 | convolution fusion | flops 464928768 | bytes 362496 | tf_op jit(solution)/shard_map/dot_general | solution.py:46
  256.7 0.6 pad_maximum_fusion
  (5 shorter events, 0.1 us)
Async XLA Ops:
  6.5 58.0 %all-gather.2.cloned.1.call-start = ((), (), s32[]{:S(2)}) async-start(), calls=%async_computation | async-start | bytes 2228224 | tf_op jit(solution)/shard_map/all_gather | solution.py:66
  7.3 68.4 %copy-start.1 = (s32[64]{0:T(128)S(1)}, s32[64]{0:T(128)}, u32[]{:S(2)}) copy-start(s32[64]{0:T(128)} %param.6) | copy-start | bytes 772
  7.3 68.5 %copy-start = (s32[512]{0:T(512)S(1)}, s32[512]{0:T(512)}, u32[]{:S(2)}) copy-start(s32[512]{0:T(512)} %param.7) | copy-start | bytes 6148
  7.3 212.3 %all-reduce.2.cloned.1.call-start = ((), (), s32[]{:S(2)}) async-start(), calls=%async_computation.1 | async-start | bytes 8388608 | tf_op jit(solution)/shard_map/psum | solution.py:77
  220.8 15.2 %collective-permute-start = (f32[4,2,4,256]{3,0,2,1:T(4,128)S(1)}, f32[4,2,4,256]{3,0,2,1:T(4,128)S(1)}, u32[]{:S(2)}, u32[]{:S(2)}) collective-permute-start(f32[4,2,4,256]{3,0,2,1:T(4,128)S(1)} %pad_maximum_fusion.1), channel_id=1, source_target_pairs={{16,0},{32,16},{48,32},{64,48},{80,64},{96,80},{112,96},{128,112},... | collective-permute-start | bytes 98312 | tf_op jit(solution)/shard_map/ppermute | solution.py:16
Sparse Core Ops, SparseCore 0:
  10.1 54.4 all-gather.1
  75.8 143.7 all-reduce.1
where the time goes:
time: 266 us; the launch traced here: 264 us
  waiting for transfers between devices  205 us (77%)
  matrix products  31.7 us (12%)
  between operations  13.5 us (5%)
  starting transfers between devices  11.2 us (4%)
    psum x1, waiting for transfers between devices, body(): summed = lax.psum(projected, 'rows')  144 us
    all_gather x1, waiting for transfers between devices, body(): block_rows = lax.all_gather(spod_modes, 'tm', axis=0, tiled=True)  57.3 us
    dot_general x1, matrix products, envelope(): lax.dot_general(flat_rows, weights, (((1,), (1,)), ((), ())), precision=l...  20.7 us
    ppermute x1, starting transfers between devices, from_behind(): return lax.ppermute(block, axis, route)  11.2 us
    dot_general x1, matrix products, body(): lax.dot_general(flat_modes, snapshots, (((1,), (1,)), ((), ())), preferre...  11 us
  transfers between devices with their start and end apart: 3, of which 3 were waited for; matrix products, arithmetic and copies ran while one was open for 0% of the time, Pallas kernels for 0%

commit v1 on v0

v1 whole, which is shorter than its diff:
```python
import math

import jax
import jax.numpy as jnp
from jax import lax
from jax.sharding import PartitionSpec as P

F = 64
M = 4
L = 256


def hann_weights(distance):
    inside = (distance >= 0) & (distance < L)
    angles = distance.astype(jnp.float32) * (2.0 * math.pi / L)
    values = math.sqrt(8.0 / (3.0 * L)) * (0.5 - 0.5 * jnp.cos(angles))
    return jnp.where(inside, values, 0.0)


def phase_pair(frequency, moments):
    phase_bin = frequency[:, None] * moments[None, :] % L
    angles = phase_bin.astype(jnp.float32) * (2.0 * math.pi / L)
    return (jnp.cos(angles)[:, None, :], jnp.sin(angles)[:, None, :])


def demodulate(projected, frequency, moments):
    cosine, sine_part = phase_pair(frequency, moments)
    real_in = projected[:, 0]
    imag_in = projected[:, 1]
    real_out = cosine * real_in - sine_part * imag_in
    imag_out = -(sine_part * real_in + cosine * imag_in)
    return jnp.stack([real_out, imag_out], 1)


def body(snapshots, spod_modes, freq_index, seg_offsets):
    time_len = snapshots.shape[0]
    tm_pos = lax.axis_index("tm")
    row_pos = lax.axis_index("rows")
    block_rows = lax.all_gather(spod_modes, "tm", axis=0, tiled=True)
    flat_modes = block_rows.reshape(F * 2 * M, block_rows.shape[3])
    partial = lax.dot_general(
        flat_modes, snapshots, (((1,), (1,)), ((), ())), preferred_element_type=jnp.float32
    )
    route = [(i + 1, i) for i in range(lax.axis_size("tm") - 1)]
    behind = lax.ppermute(partial[:, :L], "tm", route)
    moments = tm_pos * time_len + jnp.arange(time_len + L, dtype=jnp.int32)

    def windowed(part, first, length):
        shaped = part.reshape(F, 2, M, length)
        demodulated = demodulate(shaped, freq_index, moments[first:first + length])
        at = first + jnp.arange(length, dtype=jnp.int32)
        weights = hann_weights(at[:, None] - seg_offsets[None, :])
        return lax.dot_general(
            demodulated.reshape(F * 2 * M, length),
            weights,
            (((1,), (0,)), ((), ())),
            precision=lax.Precision.HIGH,
            preferred_element_type=jnp.float32,
        )

    summed = windowed(partial, 0, time_len) + windowed(behind, time_len, L)
    summed = summed.reshape(F, 2, M, seg_offsets.shape[0])
    mine = lax.psum_scatter(summed, "rows", scatter_dimension=0, tiled=True)
    share_len = F // lax.axis_size("rows")
    own_freqs = lax.dynamic_slice_in_dim(freq_index, row_pos * share_len, share_len, 0)
    cosine, sine_part = phase_pair(own_freqs, tm_pos * time_len + seg_offsets)
    env_real = mine[:, 0]
    env_imag = mine[:, 1]
    return jnp.stack(
        [cosine * env_real - sine_part * env_imag, sine_part * env_real + cosine * env_imag], 1
    )


def solution(mesh):
    placed = (P("tm", "rows"), P("tm", None, None, "rows"), P(), P("tm"))
    return jax.shard_map(
        body, mesh=mesh, in_specs=placed, out_specs=P("rows", None, None, "tm"), check_vma=False
    )
```

time: 266 us -> 269 us (1.011)
  the two profiles are of different devices: /device:TPU:27 before, /device:TPU:8 now
where the time goes in v1:
time: 269 us; the launch traced here: 268 us
  waiting for transfers between devices  192 us (71%)
  matrix products  30.4 us (11%)
  local copies, waits for them, and re-layouts  17.4 us (6%)
  between operations  14.3 us (5%)
  other arithmetic  11.5 us (4%)
  starting transfers between devices  2.82 us (1%)
    unnamed x3, waiting for transfers between devices  138 us
    all_gather x1, waiting for transfers between devices, body(): block_rows = lax.all_gather(spod_modes, 'tm', axis=0, tiled=True)  54.2 us
    dot_general x2, matrix products, windowed(): lax.dot_general(demodulated.reshape(F * 2 * M, length), weights, (((1,),...  23.4 us
    dot_general x1, matrix products, body(): lax.dot_general(flat_modes, snapshots, (((1,), (1,)), ((), ())), preferre...  6.96 us
    reshape x2, local copies, waits for them, and re-layouts, windowed(): demodulated.reshape(F * 2 * M, length)  5.51 us
  transfers between devices with their start and end apart: 3, of which 2 were waited for; matrix products, arithmetic and copies ran while one was open for 10% of the time, Pallas kernels for 0%

profile of v1, /device:TPU:8, one launch (start us, length us, event | category | flops | bytes accessed | tf_op | source)
XLA Modules:
  0.0 268.1 jit_solution(8194953738576129666)
XLA Ops:
  6.5 0.0 all-gather.2.cloned.1.call-start
  6.5 0.7 all-gather.2.cloned.1.call-update
  7.3 0.0 all-reduce.3.cloned.1.call-start
  7.4 1.0 fusion.46
  8.4 2.8 %fusion.41 = (f32[64,2048]{1,0:T(8,128)S(1)}, f32[64,2048]{1,0:T(8,128)S(1)}) fusion(s32[2048]{0:T(1024)S(1)} %slice.36, s32[64]{0:T(128)} %param.6), kind=kLoop, calls=%fused_computation.53 | loop fusion | flops 1835008 | bytes 1057024 | tf_op jit(solution)/shard_map/cos | solution.py:23
  11.1 54.2 %all-gather.2.cloned.1.call-done = bf16[64,2,4,2048]{3,2,1,0:T(4,128)(2,1)} async-done(((bf16[4,2,4,2048]{3,2,1,0:T(4,128)(2,1)}), bf16[64,2,4,2048]{3,2,1,0:T(4,128)(2,1)}) %all-gather.2.cloned.1.call-update) | async-done | bytes 2097168 | tf_op jit(solution)/shard_map/all_gather | solution.py:39
  65.3 2.5 reshape.189
  67.8 7.0 %fusion.64 = f32[512,2048]{1,0:T(8,128)S(1)} fusion(bf16[512,2048]{1,0:T(8,128)(2,1)S(1)} %reshape.189, bf16[2048,2048]{1,0:T(8,128)(2,1)} %param.4), kind=kOutput, calls=%fused_computation.92 | convolution fusion | flops 4294967296 | bytes 14680064 | tf_op jit(solution)/shard_map/dot_general | solution.py:41
  74.8 0.0 copy-start
  74.8 1.9 copy-done
  76.8 5.2 %reshape.190 = f32[64,2,4,2048]{3,2,1,0:T(4,128)} reshape(f32[512,2048]{1,0:T(8,128)} %copy-done) | data formatting | bytes 8388608 | tf_op jit(solution)/shard_map/reshape | solution.py:49
  82.0 2.9 %multiply_subtract_fusion = (f32[64,1,4,2048]{3,2,1,0:T(4,128)S(1)}, f32[64,1,4,2048]{3,2,1,0:T(4,128)S(1)}) fusion(f32[64,2,4,2048]{3,2,1,0:T(4,128)} %reshape.190, f32[64,2048]{1,0:T(8,128)S(1)} %get-tuple-element.12, f32[64,2048]{1,0:T(8,128)S(1)} %get-tuple-element.11), kind=kLoop, calls=%fused_computation.21 | loop fusion | flops 3670016 | bytes 9437184 | tf_op jit(solution)/shard_map/sub | solution.py:30
  84.9 3.0 %pad_maximum_fusion = f32[64,2,4,2048]{3,2,1,0:T(4,128)} fusion(f32[64,1,4,2048]{3,2,1,0:T(4,128)S(1)} %get-tuple-element.6, f32[64,1,4,2048]{3,2,1,0:T(4,128)S(1)} %get-tuple-element.5), kind=kLoop, calls=%fused_computation | loop fusion | flops 1048576 | bytes 8388608 | tf_op jit(solution)/shard_map/stack | solution.py:32
  87.9 0.0 copy-start.1
  87.9 5.3 %reshape.191 = f32[512,2048]{1,0:T(8,128)} reshape(f32[64,2,4,2048]{3,2,1,0:T(4,128)} %pad_maximum_fusion) | data formatting | bytes 8388608 | tf_op jit(solution)/shard_map/reshape | solution.py:54
  93.2 2.8 %collective-permute-start = (f32[512,256]{1,0:T(8,128)S(1)}, f32[512,256]{1,0:T(8,128)S(1)}, u32[]{:S(2)}, u32[]{:S(2)}) collective-permute-start(f32[512,256]{1,0:T(8,128)S(1)} %slice.40), channel_id=1, source_target_pairs={{16,0},{32,16},{48,32},{64,48},{80,64},{96,80},{112,96},{128,112},... | collective-permute-start | bytes 1572872 | tf_op jit(solution)/shard_map/ppermute | solution.py:45
  96.0 0.0 copy-done.1
  96.0 20.9 %fusion = f32[512,512]{1,0:T(8,128)S(1)} fusion(f32[512,2048]{1,0:T(8,128)} %reshape.191, s32[512]{0:T(512)S(1)} %copy-done.1), kind=kOutput, calls=%fused_computation.1 | convolution fusion | flops 3231711232 | bytes 5244928 | tf_op jit(solution)/shard_map/dot_general | solution.py:53
  117.0 0.0 collective-permute-done
  117.0 0.1 reshape.192
  117.1 0.2 multiply_subtract_fusion.1
  117.3 0.0 copy-start.2
  117.3 0.0 copy-start.3
  117.3 0.1 pad_maximum_fusion.1
  117.4 0.2 reshape.193
  117.6 2.5 convolution_add_fusion
  120.1 1.3 reshape.194
  121.4 0.0 all-reduce.3.cloned.1.call-update
  121.5 0.0 copy-done.2
  121.5 0.1 dynamic_slice.3
  121.5 0.0 copy-done.3
  121.5 0.6 dynamic-slice
  122.8 0.2 fusion.51
  122.9 136.9 %all-reduce.3.cloned.1.call-done = f32[64,2,4,512]{3,2,1,0:T(4,128)} async-done(((f32[64,2,4,512]{3,2,1,0:T(4,128)}), f32[64,2,4,512]{3,2,1,0:T(4,128)}) %all-reduce.3.cloned.1.call-update) | async-done | bytes 1048592
  259.8 0.8 multiply_subtract_fusion.2
  260.6 0.6 pad_maximum_fusion.2
  (6 shorter events, 0.1 us)
Async XLA Ops:
  6.5 58.8 %all-gather.2.cloned.1.call-start = ((), (), s32[]{:S(2)}) async-start(), calls=%async_computation | async-start | bytes 2228224 | tf_op jit(solution)/shard_map/all_gather | solution.py:39
  7.3 252.6 %all-reduce.3.cloned.1.call-start = ((), (), s32[]{:S(2)}) async-start(), calls=%async_computation.1 | async-start | bytes 2097152
  74.8 1.9 copy-start
  87.9 8.1 %copy-start.1 = (s32[512]{0:T(512)S(1)}, s32[512]{0:T(512)}, u32[]{:S(2)}) copy-start(s32[512]{0:T(512)} %param.7) | copy-start | bytes 6148
  93.2 23.7 %collective-permute-start = (f32[512,256]{1,0:T(8,128)S(1)}, f32[512,256]{1,0:T(8,128)S(1)}, u32[]{:S(2)}, u32[]{:S(2)}) collective-permute-start(f32[512,256]{1,0:T(8,128)S(1)} %slice.40), channel_id=1, source_target_pairs={{16,0},{32,16},{48,32},{64,48},{80,64},{96,80},{112,96},{128,112},... | collective-permute-start | bytes 1572872 | tf_op jit(solution)/shard_map/ppermute | solution.py:45
  117.3 4.2 %copy-start.2 = (s32[64]{0:T(128)S(1)}, s32[64]{0:T(128)}, u32[]{:S(2)}) copy-start(s32[64]{0:T(128)} %param.6) | copy-start | bytes 772
  117.3 4.2 %copy-start.3 = (u32[256]{0:T(256)S(1)}, u32[256]{0:T(256)}, u32[]{:S(2)}) copy-start(u32[256]{0:T(256)} %constant.67) | copy-start | bytes 3076
Sparse Core Ops, SparseCore 0:
  10.1 55.1 all-gather.1
  121.6 138.2 all-reduce.2

commit v2 on v1

v2 whole, which is shorter than its diff:
```python
import functools
import math

import jax
import jax.numpy as jnp
from jax import lax
from jax.experimental import pallas as pl
from jax.experimental.pallas import tpu as pltpu
from jax.sharding import PartitionSpec as P

F = 64
M = 4
L = 256
T = 2048
S = 512
R = 2048
BLOCK = 32
HALF = 256
TILES = T // L
SCALE = 2.0 * math.pi / L
PEAK = math.sqrt(8.0 / (3.0 * L))
MESH = pl.DeviceIdType.MESH
NT = (((1,), (1,)), ((), ()))


def swap_parts(x):
    rows, cols = x.shape
    return pltpu.roll(x.reshape(rows // 8, 8, cols), 4, 1).reshape(rows, cols)


def split(x):
    high = x.astype(jnp.bfloat16)
    return high, (x - high.astype(jnp.float32)).astype(jnp.bfloat16)


def dot(a, b):
    return jnp.dot(a, b, preferred_element_type=jnp.float32)


def kernel(
    freq_ref, snap_hbm, modes_hbm, off_ref, out_ref,
    snap, modes, d_high, d_low, w_high, w_low, turn, cross, hann, out_turn, out_cross,
    part, landed, total, other,
    snap_sem, own_sem, ag_send, ag_recv, edge_send, edge_recv, rs_send, rs_recv, x_send, x_recv,
):
    tm = lax.axis_index("tm")
    rows = lax.axis_index("rows")
    hi, y, core = tm // 8, (tm // 2) % 4, tm % 2
    lo, z = rows // 8, rows % 8
    way = 1 - 2 * core

    def block_id(h, yy, c):
        return h * 8 + (yy % 4) * 2 + c

    def at(b):
        return modes.at[b // 8, pl.ds(pl.multiple_of((b % 8) * BLOCK, BLOCK), BLOCK), :]

    snap_copy = pltpu.make_async_copy(snap_hbm, snap, snap_sem)
    snap_copy.start()
    own_copy = pltpu.make_async_copy(modes_hbm, at(tm), own_sem)
    own_copy.start()

    mate = block_id(hi, y, 1 - core)
    near = [block_id(hi, y + 1, core), block_id(hi, y + 3, core), block_id(hi, y + 2, core)]
    far = [block_id(1 - hi, y + k, core) for k in (0, 1, 3, 2)]
    below = (tm + 15) % 16
    above = (tm + 1) % 16
    cross_edge = jnp.where(core == 0, below, above)
    z_next = lo * 8 + (z + 8 + way) % 8
    z_prev = lo * 8 + (z + 8 - way) % 8
    x_mate = (1 - lo) * 8 + z

    barrier = pltpu.get_barrier_semaphore()
    for b in [mate, cross_edge] + near + far:
        pl.semaphore_signal(barrier, inc=1, device_id=(b, rows), device_id_type=MESH)
    for r in (z_next, z_prev, x_mate):
        pl.semaphore_signal(barrier, inc=1, device_id=(tm, r), device_id_type=MESH)
    pl.semaphore_wait(barrier, 12)

    sends = []

    def send(src, dst, send_sem, recv_sem, to):
        copy = pltpu.make_async_remote_copy(
            src_ref=src, dst_ref=dst, send_sem=send_sem, recv_sem=recv_sem, device_id=to, device_id_type=MESH
        )
        copy.start()
        sends.append(copy)

    def arrived(dst, recv_sem, to):
        pltpu.make_async_remote_copy(
            src_ref=dst, dst_ref=dst, send_sem=recv_sem, recv_sem=recv_sem, device_id=to, device_id_type=MESH
        ).wait_recv()

    for n, b in enumerate([mate] + near + far):
        send(modes_hbm, at(tm), ag_send.at[n], ag_recv.at[tm], (b, rows))

    def hand_on(n, b):
        arrived(at(b), ag_recv.at[b], (b, rows))
        send(at(b), at(b), ag_send.at[8 + n], ag_recv.at[b], (mate, rows))

    lane = lax.broadcasted_iota(jnp.int32, (8, L), 1)
    upper = lax.broadcasted_iota(jnp.int32, (8, L), 0) < 4

    @pl.loop(0, F, unroll=4)
    def _(f):
        angle = ((freq_ref[f] * lane) & (L - 1)).astype(jnp.float32) * SCALE
        cosine = jnp.cos(angle)
        at_rows = pl.ds(pl.multiple_of((f % 32) * 8, 8), 8)
        turn[f // 32, at_rows, :] = jnp.where(upper, cosine, -cosine)
        cross[f // 32, at_rows, :] = -jnp.sin(angle)

    offsets = off_ref[...]
    upper_out = lax.broadcasted_iota(jnp.int32, (8, S), 0) < 4
    for q in range(4):
        bins = (freq_ref[rows * 4 + q] * jnp.broadcast_to(offsets, (8, S))) & (L - 1)
        angle = bins.astype(jnp.float32) * SCALE
        sine = jnp.sin(angle)
        out_turn[pl.ds(q * 8, 8), :] = jnp.cos(angle)
        out_cross[pl.ds(q * 8, 8), :] = jnp.where(upper_out, -sine, sine)

    for n in range(3):
        hand_on(n, near[n])

    within = offsets & (L - 1)
    tile_of = offsets // L

    @pl.loop(0, L // 32)
    def _(k):
        moment = k * 32 + lax.broadcasted_iota(jnp.int32, (32, S), 0)
        angle = ((moment - within) & (L - 1)).astype(jnp.float32) * SCALE
        hann[pl.ds(pl.multiple_of(k * 32, 32), 32), :] = PEAK * (0.5 - 0.5 * jnp.cos(angle))

    @pl.loop(0, TILES + 1)
    def _(tile):
        @pl.loop(0, L // 32)
        def _(k):
            moment = k * 32 + lax.broadcasted_iota(jnp.int32, (32, S), 0)
            start_tile = jnp.where(moment >= within, tile_of, tile_of + 1)
            values = hann[pl.ds(pl.multiple_of(k * 32, 32), 32), :]
            high, low = split(jnp.where(start_tile == tile, values, 0.0))
            here = pl.ds(pl.multiple_of(tile * L + k * 32, 32), 32)
            w_high[here, :] = high
            w_low[here, :] = low

    own_copy.wait()
    snap_copy.wait()
    arrived(at(mate), ag_recv.at[mate], (mate, rows))
    for k in (1, 3, 2):
        b = block_id(hi, y + k, 1 - core)
        arrived(at(b), ag_recv.at[b], (mate, rows))

    def edge_at(ref, half, tile):
        return ref.at[half, :, pl.ds(tile * L, L)]

    def project(k, tile):
        half = hi if k == 0 else 1 - hi
        p = lax.dot_general(
            modes[half], snap[pl.ds(tile * L, L), :], NT, preferred_element_type=jnp.float32
        )
        high, low = split(turn[half] * p + cross[half] * swap_parts(p))
        d_high[half, :, pl.ds(tile * L, L)] = high
        d_low[half, :, pl.ds(tile * L, L)] = low
        if tile == 0:
            @pl.when(tm > 0)
            def _():
                for n, ref in enumerate((d_high, d_low)):
                    pltpu.make_async_remote_copy(
                        src_ref=edge_at(ref, half, 0), dst_ref=edge_at(ref, half, TILES),
                        send_sem=edge_send.at[half, n], recv_sem=edge_recv.at[half, n],
                        device_id=(below, rows), device_id_type=MESH,
                    ).start()

    def window(k):
        half = hi if k == 0 else 1 - hi

        def sums(first, length, cols):
            at_t = pl.ds(first, length)
            high = d_high[half, :, at_t]
            return (
                dot(high, w_high[at_t, cols])
                + dot(d_low[half, :, at_t], w_high[at_t, cols])
                + dot(high, w_low[at_t, cols])
            )

        for n in range(2):
            cols = pl.ds(n * 256, 256)
            part[k, :, cols] = sums(0, T, cols)

        @pl.when(tm < 15)
        def _():
            for n, ref in enumerate((d_high, d_low)):
                arrived(edge_at(ref, half, TILES), edge_recv.at[half, n], (above, rows))
            part[k] += sums(T, L, pl.ds(0, S))

    def dest(d):
        return pl.ds(pl.multiple_of(((z + 8 + d) % 8) * BLOCK, BLOCK), BLOCK)

    def chain_send(k, n, d, to):
        send(part.at[k, dest(d), :], landed.at[k, n], rs_send.at[k, n], rs_recv.at[k, n], (tm, to))

    def chain_wait(k, n, to):
        arrived(landed.at[k, n], rs_recv.at[k, n], (tm, to))

    def reduce_step(k, step):
        if step == 0:
            chain_send(k, 0, 4 * way, z_next)
            chain_send(k, 4, -3 * way, z_prev)
            return
        chain_wait(k, step - 1, z_prev)
        if step < 4:
            d = (4 - step) * way
            part[k, dest(d), :] += landed[k, step - 1]
            chain_send(k, step, d, z_next)
            chain_wait(k, 3 + step, z_next)
            if step < 3:
                d = (step - 3) * way
                part[k, dest(d), :] += landed[k, 3 + step]
                chain_send(k, 4 + step, d, z_prev)
            return
        total[k] = part[k, dest(0), :] + landed[k, 3] + landed[k, 6]
        half = hi if k == 0 else 1 - hi

        @pl.when(lo != half)
        def _():
            pltpu.make_async_remote_copy(
                src_ref=total.at[k], dst_ref=other, send_sem=x_send, recv_sem=x_recv,
                device_id=(tm, x_mate), device_id_type=MESH,
            ).start()

    for tile in range(TILES):
        project(0, tile)
        if tile == 2:
            for n in range(3):
                hand_on(3 + n, far[n])
        if tile == 5:
            hand_on(6, far[3])
    window(0)
    reduce_step(0, 0)
    for k in (0, 1, 3, 2):
        b = block_id(1 - hi, y + k, 1 - core)
        arrived(at(b), ag_recv.at[b], (mate, rows))
    for tile in range(TILES):
        project(1, tile)
        if tile % 2 == 1:
            reduce_step(0, tile // 2 + 1)
    window(1)
    for step in range(5):
        reduce_step(1, step)

    arrived(other, x_recv, (tm, x_mate))
    mine = jnp.where(lo == hi, 0, 1)
    env = total[mine] + other[...]
    out_ref[...] = out_turn[...] * env + out_cross[...] * swap_parts(env)

    for copy in sends:
        copy.wait_send()

    @pl.when(tm > 0)
    def _():
        for half in range(2):
            for n, ref in enumerate((d_high, d_low)):
                pltpu.make_async_remote_copy(
                    src_ref=edge_at(ref, half, 0), dst_ref=edge_at(ref, half, TILES),
                    send_sem=edge_send.at[half, n], recv_sem=edge_recv.at[half, n],
                    device_id=(below, rows), device_id_type=MESH,
                ).wait_send()

    pltpu.make_async_remote_copy(
        src_ref=total.at[1 - mine], dst_ref=other, send_sem=x_send, recv_sem=x_recv,
        device_id=(tm, x_mate), device_id_type=MESH,
    ).wait_send()


def body(snapshots, spod_modes, freq_index, seg_offsets):
    bf16, f32 = jnp.bfloat16, jnp.float32
    vmem = pltpu.VMEM
    dma = pltpu.SemaphoreType.DMA
    out = pl.pallas_call(
        kernel,
        out_shape=jax.ShapeDtypeStruct((BLOCK, S), f32),
        in_specs=[
            pl.BlockSpec(memory_space=pltpu.SMEM),
            pl.BlockSpec(memory_space=pl.ANY),
            pl.BlockSpec(memory_space=pl.ANY),
            pl.BlockSpec(memory_space=vmem),
        ],
        out_specs=pl.BlockSpec(memory_space=vmem),
        scratch_shapes=[
            vmem((T, R), bf16),
            vmem((2, HALF, R), bf16),
            vmem((2, HALF, T + L), bf16),
            vmem((2, HALF, T + L), bf16),
            vmem((T + L, S), bf16),
            vmem((T + L, S), bf16),
            vmem((2, HALF, L), f32),
            vmem((2, HALF, L), f32),
            vmem((L, S), f32),
            vmem((BLOCK, S), f32),
            vmem((BLOCK, S), f32),
            vmem((2, HALF, S), f32),
            vmem((2, 7, BLOCK, S), f32),
            vmem((2, BLOCK, S), f32),
            vmem((BLOCK, S), f32),
            dma, dma,
            dma((15,)), dma((16,)),
            dma((2, 2)), dma((2, 2)),
            dma((2, 7)), dma((2, 7)),
            dma, dma,
        ],
        compiler_params=pltpu.CompilerParams(
            collective_id=0, has_side_effects=True, vmem_limit_bytes=56 * 1024 * 1024
        ),
        cost_estimate=pl.CostEstimate(flops=8 * 10**9, bytes_accessed=10**7, transcendentals=0),
    )(freq_index, snapshots, spod_modes.reshape(BLOCK, R), seg_offsets.reshape(1, S))
    return out.reshape(F // 16, 2, M, S)


def solution(mesh):
    placed = (P("tm", "rows"), P("tm", None, None, "rows"), P(), P("tm"))
    return jax.shard_map(
        body, mesh=mesh, in_specs=placed, out_specs=P("rows", None, None, "tm"), check_vma=False
    )
```

time: 269 us -> 67.5 us (0.25)
  the two profiles are of different devices: /device:TPU:8 before, /device:TPU:27 now
where the time goes in v2:
time: 67.5 us; the launch traced here: 67.1 us
  Pallas kernels  64.1 us (95%)
  local copies, waits for them, and re-layouts  3.06 us (5%)
    pallas_call x1, Pallas kernels, body(): pl.pallas_call(kernel, out_shape=jax.ShapeDtypeStruct((BLOCK, S), f32), i...  64.1 us
    reshape x1, local copies, waits for them, and re-layouts, body(): spod_modes.reshape(BLOCK, R)  1.57 us
    reshape x1, local copies, waits for them, and re-layouts, body(): return out.reshape(F // 16, 2, M, S)  1.49 us

profile of v2, /device:TPU:27, one launch (start us, length us, event | category | flops | bytes accessed | tf_op | source)
XLA Modules:
  0.0 67.1 jit_solution(14196186491481396291)
XLA Ops:
  0.0 1.6 %reshape.9.modes_hbm = bf16[32,2048]{1,0:T(8,128)(2,1)} reshape(bf16[4,2,4,2048]{3,2,1,0:T(4,128)(2,1)} %param.5) | data formatting | bytes 262144 | tf_op jit(solution)/shard_map/reshape | solution.py:314
  1.6 64.1 %shard_map.46 = f32[32,512]{1,0:T(8,128)} custom-call(s32[64]{0:T(128)} %freq_ref.1, bf16[2048,2048]{1,0:T(8,128)(2,1)} %snap_hbm.1, bf16[32,2048]{1,0:T(8,128)(2,1)} %reshape.9.modes_hbm, s32[1,512]{1,0:T(1,128)} %bitcast.1), custom_call_target="tpu_custom_call" | custom-call | flops 8000000000 | bytes 10000000 | tf_op jit(solution)/shard_map/pallas_call | solution.py:278
  65.6 1.5 %reshape.11 = f32[4,2,4,512]{3,2,1,0:T(4,128)} reshape(f32[32,512]{1,0:T(8,128)} %shard_map.46) | data formatting | bytes 131072 | tf_op jit(solution)/shard_map/reshape | solution.py:315

commit v3 on v2

v3 whole, which is shorter than its diff:
```python
import functools
import math

import jax
import jax.numpy as jnp
from jax import lax
from jax.experimental import pallas as pl
from jax.experimental.pallas import tpu as pltpu
from jax.sharding import PartitionSpec as P

F = 64
M = 4
L = 256
T = 2048
S = 512
R = 2048
BLOCK = 32
HALF = 256
TILES = T // L
SCALE = 2.0 * math.pi / L
PEAK = math.sqrt(8.0 / (3.0 * L))
MESH = pl.DeviceIdType.MESH
NT = (((1,), (1,)), ((), ()))


def swap_parts(x):
    rows, cols = x.shape
    return pltpu.roll(x.reshape(rows // 8, 8, cols), 4, 1).reshape(rows, cols)


def split(x):
    high = x.astype(jnp.bfloat16)
    return high, (x - high.astype(jnp.float32)).astype(jnp.bfloat16)


def dot(a, b):
    return jnp.dot(a, b, preferred_element_type=jnp.float32)


def kernel(
    freq_ref, snap_hbm, modes_hbm, off_ref, out_ref,
    snap, modes, d_high, d_low, w_high, w_low, turn, cross, hann, out_turn, out_cross,
    part, landed, total, other, raw,
    snap_sem, own_sem, ag_send, ag_recv, edge_send, edge_recv, rs_send, rs_recv, x_send, x_recv,
):
    tm = lax.axis_index("tm")
    rows = lax.axis_index("rows")
    hi, y, core = tm // 8, (tm // 2) % 4, tm % 2
    lo, z = rows // 8, rows % 8
    way = 1 - 2 * core

    def block_id(h, yy, c):
        return h * 8 + (yy % 4) * 2 + c

    def at(b):
        return modes.at[b // 8, pl.ds(pl.multiple_of((b % 8) * BLOCK, BLOCK), BLOCK), :]

    snap_copy = pltpu.make_async_copy(snap_hbm, snap, snap_sem)
    snap_copy.start()
    own_copy = pltpu.make_async_copy(modes_hbm, raw, own_sem)
    own_copy.start()

    mate = block_id(hi, y, 1 - core)
    up, down, opposite = [block_id(hi, y + k, core) for k in (1, 3, 2)]
    peer, peer_up, peer_down, peer_opposite = [block_id(1 - hi, y + k, core) for k in (0, 1, 3, 2)]
    below = (tm + 15) % 16
    above = (tm + 1) % 16
    cross_edge = jnp.where(core == 0, below, above)
    z_next = lo * 8 + (z + 8 + way) % 8
    z_prev = lo * 8 + (z + 8 - way) % 8
    x_mate = (1 - lo) * 8 + z

    barrier = pltpu.get_barrier_semaphore()
    for b in (mate, cross_edge, up, down, peer):
        pl.semaphore_signal(barrier, inc=1, device_id=(b, rows), device_id_type=MESH)
    for r in (z_next, z_prev, x_mate):
        pl.semaphore_signal(barrier, inc=1, device_id=(tm, r), device_id_type=MESH)

    lane = lax.broadcasted_iota(jnp.int32, (8, L), 1)
    upper = lax.broadcasted_iota(jnp.int32, (8, L), 0) < 4

    @pl.loop(0, F, unroll=4)
    def _(f):
        angle = ((freq_ref[f] * lane) & (L - 1)).astype(jnp.float32) * SCALE
        cosine = jnp.cos(angle)
        at_rows = pl.ds(pl.multiple_of((f % 32) * 8, 8), 8)
        turn[f // 32, at_rows, :] = jnp.where(upper, cosine, -cosine)
        cross[f // 32, at_rows, :] = -jnp.sin(angle)

    offsets = off_ref[...]
    upper_out = lax.broadcasted_iota(jnp.int32, (8, S), 0) < 4
    for q in range(4):
        bins = (freq_ref[rows * 4 + q] * jnp.broadcast_to(offsets, (8, S))) & (L - 1)
        angle = bins.astype(jnp.float32) * SCALE
        sine = jnp.sin(angle)
        out_turn[pl.ds(q * 8, 8), :] = jnp.cos(angle)
        out_cross[pl.ds(q * 8, 8), :] = jnp.where(upper_out, -sine, sine)

    within = offsets & (L - 1)
    tile_of = offsets // L

    @pl.loop(0, L // 32)
    def _(k):
        moment = k * 32 + lax.broadcasted_iota(jnp.int32, (32, S), 0)
        angle = ((moment - within) & (L - 1)).astype(jnp.float32) * SCALE
        hann[pl.ds(pl.multiple_of(k * 32, 32), 32), :] = PEAK * (0.5 - 0.5 * jnp.cos(angle))

    @pl.loop(0, TILES + 1)
    def _(tile):
        @pl.loop(0, L // 32)
        def _(k):
            moment = k * 32 + lax.broadcasted_iota(jnp.int32, (32, S), 0)
            start_tile = jnp.where(moment >= within, tile_of, tile_of + 1)
            values = hann[pl.ds(pl.multiple_of(k * 32, 32), 32), :]
            high, low = split(jnp.where(start_tile == tile, values, 0.0))
            here = pl.ds(pl.multiple_of(tile * L + k * 32, 32), 32)
            w_high[here, :] = high
            w_low[here, :] = low

    own_copy.wait()
    own = at(tm)
    for n in range(2):
        pair = [raw[2 * n + q].astype(jnp.float32).reshape(8, R) for q in range(2)]
        own[pl.ds(n * 16, 16), :] = jnp.concatenate(pair, 0).astype(jnp.bfloat16)

    pl.semaphore_wait(barrier, 8)

    sends = []

    def send(src, dst, send_sem, recv_sem, to):
        copy = pltpu.make_async_remote_copy(
            src_ref=src, dst_ref=dst, send_sem=send_sem, recv_sem=recv_sem, device_id=to, device_id_type=MESH
        )
        copy.start()
        sends.append(copy)

    def arrived(dst, recv_sem, to):
        pltpu.make_async_remote_copy(
            src_ref=dst, dst_ref=dst, send_sem=recv_sem, recv_sem=recv_sem, device_id=to, device_id_type=MESH
        ).wait_recv()

    def piece_at(b, piece):
        return modes.at[b // 8, pl.ds(pl.multiple_of((b % 8) * BLOCK + piece * 16, 16), 16), :]

    def send_block(n, b, to):
        send(at(b), at(b), ag_send.at[n], ag_recv.at[b, 0], (to, rows))

    def send_piece(n, b, piece, to):
        here = piece_at(b, piece)
        send(here, here, ag_send.at[n], ag_recv.at[b, piece], (to, rows))

    def block_arrived(b, source):
        arrived(at(b), ag_recv.at[b, 0], (source, rows))

    def piece_arrived(b, piece, source):
        arrived(piece_at(b, piece), ag_recv.at[b, piece], (source, rows))

    send_block(0, tm, peer)
    send_block(1, tm, up)
    send_block(2, tm, down)
    send_block(3, tm, mate)
    block_arrived(up, up)
    send_piece(4, up, 0, down)
    block_arrived(down, down)
    send_piece(5, down, 1, up)
    send_block(6, up, mate)
    send_block(7, down, mate)
    block_arrived(peer, peer)
    send_block(8, peer, up)
    send_block(9, peer, down)
    send_block(10, peer, mate)
    piece_arrived(opposite, 0, up)
    send_piece(11, opposite, 0, peer)
    piece_arrived(opposite, 1, down)
    send_piece(12, opposite, 1, peer)
    send_block(13, opposite, mate)

    snap_copy.wait()
    for k in (0, 1, 3, 2):
        block_arrived(block_id(hi, y + k, 1 - core), mate)

    def edge_at(ref, half, tile):
        return ref.at[half, :, pl.ds(tile * L, L)]

    def project(k, tile):
        half = hi if k == 0 else 1 - hi
        p = lax.dot_general(
            modes[half], snap[pl.ds(tile * L, L), :], NT, preferred_element_type=jnp.float32
        )
        high, low = split(turn[half] * p + cross[half] * swap_parts(p))
        d_high[half, :, pl.ds(tile * L, L)] = high
        d_low[half, :, pl.ds(tile * L, L)] = low
        if tile == 0:
            @pl.when(tm > 0)
            def _():
                for n, ref in enumerate((d_high, d_low)):
                    pltpu.make_async_remote_copy(
                        src_ref=edge_at(ref, half, 0), dst_ref=edge_at(ref, half, TILES),
                        send_sem=edge_send.at[half, n], recv_sem=edge_recv.at[half, n],
                        device_id=(below, rows), device_id_type=MESH,
                    ).start()

    def sums(half, first, length, cols):
        at_t = pl.ds(first, length)
        high = d_high[half, :, at_t]
        return (
            dot(high, w_high[at_t, cols])
            + dot(d_low[half, :, at_t], w_high[at_t, cols])
            + dot(high, w_low[at_t, cols])
        )

    def half_of(k):
        return hi if k == 0 else 1 - hi

    def columns(n):
        return pl.ds(n * 256, 256)

    def window(k, n):
        part[k, :, columns(n)] = sums(half_of(k), 0, T, columns(n))

    def edge_arrived(k):
        @pl.when(tm < 15)
        def _():
            for n, ref in enumerate((d_high, d_low)):
                arrived(edge_at(ref, half_of(k), TILES), edge_recv.at[half_of(k), n], (above, rows))

    def window_edge(k, n):
        @pl.when(tm < 15)
        def _():
            part[k, :, columns(n)] += sums(half_of(k), T, L, columns(n))

    def dest(d):
        return pl.ds(pl.multiple_of(((z + 8 + d) % 8) * BLOCK, BLOCK), BLOCK)

    def chain_send(k, n, i, d, to):
        send(
            part.at[k, dest(d), columns(n)], landed.at[k, n, i], rs_send.at[k, n, i], rs_recv.at[k, n, i], (tm, to)
        )

    def chain_add(k, n, i, d, source):
        arrived(landed.at[k, n, i], rs_recv.at[k, n, i], (tm, source))
        part[k, dest(d), columns(n)] += landed[k, n, i]

    def reduce_step(k, n, step):
        if step > 0:
            chain_add(k, n, step - 1, (4 - step) * way, z_prev)
        if step < 4:
            chain_send(k, n, step, (4 - step) * way, z_next)
            if step > 0:
                chain_add(k, n, 3 + step, (step - 3) * way, z_next)
            if step < 3:
                chain_send(k, n, 4 + step, (step - 3) * way, z_prev)
            return
        total[k, n] = part[k, dest(0), columns(n)]

        @pl.when(lo != half_of(k))
        def _():
            pltpu.make_async_remote_copy(
                src_ref=total.at[k, n], dst_ref=other.at[n], send_sem=x_send.at[n], recv_sem=x_recv.at[n],
                device_id=(tm, x_mate), device_id_type=MESH,
            ).start()

    for tile in range(TILES):
        project(0, tile)
        if tile == 4:
            for n, b in enumerate((peer_up, peer_down)):
                block_arrived(b, (up, down)[n])
                send_block(14 + n, b, mate)
    for piece in range(2):
        piece_arrived(peer_opposite, piece, peer)
    send_block(16, peer_opposite, mate)
    for n in range(2):
        window(0, n)
    for k in (0, 1, 3, 2):
        block_arrived(block_id(1 - hi, y + k, 1 - core), mate)
    project(1, 0)
    project(1, 1)
    edge_arrived(0)
    for n in range(2):
        window_edge(0, n)
        reduce_step(0, n, 0)
    for tile in range(2, TILES):
        project(1, tile)
    for n in range(2):
        reduce_step(0, n, 1)
    edge_arrived(1)
    for n in range(2):
        window(1, n)
        window_edge(1, n)
        reduce_step(1, n, 0)
        for m in range(2):
            reduce_step(0, m, 2 + n)
    for n in range(2):
        reduce_step(0, n, 4)
    for step in range(1, 5):
        for n in range(2):
            reduce_step(1, n, step)

    mine = jnp.where(lo == hi, 0, 1)
    for n in range(2):
        arrived(other.at[n], x_recv.at[n], (tm, x_mate))
        env = total[mine, n] + other[n]
        result = out_turn[:, columns(n)] * env + out_cross[:, columns(n)] * swap_parts(env)
        for q in range(4):
            for p in range(2):
                out_ref[q, p, :, columns(n)] = result[q * 8 + p * 4:q * 8 + p * 4 + 4]

    for copy in sends:
        copy.wait_send()

    @pl.when(tm > 0)
    def _():
        for half in range(2):
            for n, ref in enumerate((d_high, d_low)):
                pltpu.make_async_remote_copy(
                    src_ref=edge_at(ref, half, 0), dst_ref=edge_at(ref, half, TILES),
                    send_sem=edge_send.at[half, n], recv_sem=edge_recv.at[half, n],
                    device_id=(below, rows), device_id_type=MESH,
                ).wait_send()

    for n in range(2):
        pltpu.make_async_remote_copy(
            src_ref=total.at[1 - mine, n], dst_ref=other.at[n], send_sem=x_send.at[n], recv_sem=x_recv.at[n],
            device_id=(tm, x_mate), device_id_type=MESH,
        ).wait_send()


def body(snapshots, spod_modes, freq_index, seg_offsets):
    bf16, f32 = jnp.bfloat16, jnp.float32
    vmem = pltpu.VMEM
    dma = pltpu.SemaphoreType.DMA
    return pl.pallas_call(
        kernel,
        out_shape=jax.ShapeDtypeStruct((F // 16, 2, M, S), f32),
        in_specs=[
            pl.BlockSpec(memory_space=pltpu.SMEM),
            pl.BlockSpec(memory_space=pl.ANY),
            pl.BlockSpec(memory_space=pl.ANY),
            pl.BlockSpec(memory_space=vmem),
        ],
        out_specs=pl.BlockSpec(memory_space=vmem),
        scratch_shapes=[
            vmem((T, R), bf16),
            vmem((2, HALF, R), bf16),
            vmem((2, HALF, T + L), bf16),
            vmem((2, HALF, T + L), bf16),
            vmem((T + L, S), bf16),
            vmem((T + L, S), bf16),
            vmem((2, HALF, L), f32),
            vmem((2, HALF, L), f32),
            vmem((L, S), f32),
            vmem((BLOCK, S), f32),
            vmem((BLOCK, S), f32),
            vmem((2, HALF, S), f32),
            vmem((2, 2, 7, BLOCK, 256), f32),
            vmem((2, 2, BLOCK, 256), f32),
            vmem((2, BLOCK, 256), f32),
            vmem((F // 16, 2, M, R), bf16),
            dma, dma,
            dma((17,)), dma((16, 2)),
            dma((2, 2)), dma((2, 2)),
            dma((2, 2, 7)), dma((2, 2, 7)),
            dma((2,)), dma((2,)),
        ],
        compiler_params=pltpu.CompilerParams(
            collective_id=0, has_side_effects=True, vmem_limit_bytes=56 * 1024 * 1024
        ),
        cost_estimate=pl.CostEstimate(flops=8 * 10**9, bytes_accessed=10**7, transcendentals=0),
    )(freq_index, snapshots, spod_modes, seg_offsets.reshape(1, S))


def solution(mesh):
    placed = (P("tm", "rows"), P("tm", None, None, "rows"), P(), P("tm"))
    return jax.shard_map(
        body, mesh=mesh, in_specs=placed, out_specs=P("rows", None, None, "tm"), check_vma=False
    )
```

time: 67.5 us -> 60.2 us (0.89)
  Pallas kernels: 64.1 us -> 57.7 us
  local copies, waits for them, and re-layouts: 3.06 us -> 1.47 us
    pallas_call x1, Pallas kernels: 64.1 us -> 57.7 us  [body(): pl.pallas_call(kernel, out_shape=jax.ShapeDtypeStruct((F // 16, 2, M, S),...]
    reshape x2 -> x0, local copies, waits for them, and re-layouts: 3.06 us -> none  [the longest x1 1.57 us: body(): spod_modes.reshape(BLOCK, R)]
    unnamed x0 -> x1, local copies, waits for them, and re-layouts: none -> 1.47 us
where the time goes in v3:
time: 60.2 us; the launch traced here: 59.2 us
  Pallas kernels  57.7 us (96%)
  local copies, waits for them, and re-layouts  1.47 us (2%)
    pallas_call x1, Pallas kernels, body(): pl.pallas_call(kernel, out_shape=jax.ShapeDtypeStruct((F // 16, 2, M, S),...  57.7 us
    unnamed x1, local copies, waits for them, and re-layouts  1.47 us

profile of v3, /device:TPU:27, one launch (start us, length us, event | category | flops | bytes accessed | tf_op | source)
XLA Modules:
  0.0 59.2 jit_solution(15244263522061877763)
XLA Ops:
  0.0 57.7 %shard_map.46 = f32[4,2,4,512]{3,2,1,0:T(4,128)} custom-call(s32[64]{0:T(128)} %freq_ref.1, bf16[2048,2048]{1,0:T(8,128)(2,1)} %snap_hbm.1, bf16[4,2,4,2048]{3,2,1,0:T(4,128)(2,1)} %modes_hbm.1, s32[1,512]{1,0:T(1,128)} %bitcast.1), custom_call_target="tpu_custom_call" | custom-call | flops 8000000000 | bytes 10000000 | tf_op jit(solution)/shard_map/pallas_call | solution.py:332
  57.7 1.5 %copy.6 = f32[4,2,4,512]{3,2,1,0:T(4,128)} copy(f32[4,2,4,512]{3,2,1,0:T(4,128)} %shard_map.46) | data formatting | bytes 131072

commit v4 on v3

--- a/solution.py
+++ b/solution.py
@@ -19,6 +19,7 @@
 TILES = T // L
 SCALE = 2.0 * math.pi / L
 PEAK = math.sqrt(8.0 / (3.0 * L))
+CODES = 32767.0
 MESH = pl.DeviceIdType.MESH
 NT = (((1,), (1,)), ((), ()))
 
@@ -40,14 +41,13 @@
 def kernel(
     freq_ref, snap_hbm, modes_hbm, off_ref, out_ref,
     snap, modes, d_high, d_low, w_high, w_low, turn, cross, hann, out_turn, out_cross,
-    part, landed, total, other, raw,
-    snap_sem, own_sem, ag_send, ag_recv, edge_send, edge_recv, rs_send, rs_recv, x_send, x_recv,
+    part, codes, landed, raw, total,
+    snap_sem, own_sem, ag_send, ag_recv, edge_send, edge_recv, rs_send, rs_recv,
 ):
     tm = lax.axis_index("tm")
     rows = lax.axis_index("rows")
     hi, y, core = tm // 8, (tm // 2) % 4, tm % 2
     lo, z = rows // 8, rows % 8
-    way = 1 - 2 * core
 
     def block_id(h, yy, c):
         return h * 8 + (yy % 4) * 2 + c
@@ -66,15 +66,12 @@
     below = (tm + 15) % 16
     above = (tm + 1) % 16
     cross_edge = jnp.where(core == 0, below, above)
-    z_next = lo * 8 + (z + 8 + way) % 8
-    z_prev = lo * 8 + (z + 8 - way) % 8
-    x_mate = (1 - lo) * 8 + z
 
     barrier = pltpu.get_barrier_semaphore()
-    for b in (mate, cross_edge, up, down, peer):
+    for b in (mate, cross_edge, up, down, opposite, peer):
         pl.semaphore_signal(barrier, inc=1, device_id=(b, rows), device_id_type=MESH)
-    for r in (z_next, z_prev, x_mate):
-        pl.semaphore_signal(barrier, inc=1, device_id=(tm, r), device_id_type=MESH)
+    for d in range(1, 16):
+        pl.semaphore_signal(barrier, inc=1, device_id=(tm, (rows + d) % 16), device_id_type=MESH)
 
     lane = lax.broadcasted_iota(jnp.int32, (8, L), 1)
     upper = lax.broadcasted_iota(jnp.int32, (8, L), 0) < 4
@@ -123,7 +120,7 @@
         pair = [raw[2 * n + q].astype(jnp.float32).reshape(8, R) for q in range(2)]
         own[pl.ds(n * 16, 16), :] = jnp.concatenate(pair, 0).astype(jnp.bfloat16)
 
-    pl.semaphore_wait(barrier, 8)
+    pl.semaphore_wait(barrier, 21)
 
     sends = []
 
@@ -139,44 +136,31 @@
             src_ref=dst, dst_ref=dst, send_sem=recv_sem, recv_sem=recv_sem, device_id=to, device_id_type=MESH
         ).wait_recv()
 
-    def piece_at(b, piece):
-        return modes.at[b // 8, pl.ds(pl.multiple_of((b % 8) * BLOCK + piece * 16, 16), 16), :]
-
     def send_block(n, b, to):
-        send(at(b), at(b), ag_send.at[n], ag_recv.at[b, 0], (to, rows))
-
-    def send_piece(n, b, piece, to):
-        here = piece_at(b, piece)
-        send(here, here, ag_send.at[n], ag_recv.at[b, piece], (to, rows))
+        send(at(b), at(b), ag_send.at[n], ag_recv.at[b], (to, rows))
 
     def block_arrived(b, source):
-        arrived(at(b), ag_recv.at[b, 0], (source, rows))
-
-    def piece_arrived(b, piece, source):
-        arrived(piece_at(b, piece), ag_recv.at[b, piece], (source, rows))
-
-    send_block(0, tm, peer)
-    send_block(1, tm, up)
-    send_block(2, tm, down)
-    send_block(3, tm, mate)
+        arrived(at(b), ag_recv.at[b], (source, rows))
+
+    send_block(0, tm, opposite)
+    send_block(1, tm, peer)
+    send_block(2, tm, up)
+    send_block(3, tm, down)
+    send_block(4, tm, mate)
+    block_arrived(opposite, opposite)
+    send_block(5, opposite, peer)
+    block_arrived(peer, peer)
+    send_block(6, peer, up)
+    send_block(7, peer, down)
+    send_block(8, opposite, mate)
     block_arrived(up, up)
-    send_piece(4, up, 0, down)
+    send_block(9, up, mate)
     block_arrived(down, down)
-    send_piece(5, down, 1, up)
-    send_block(6, up, mate)
-    send_block(7, down, mate)
-    block_arrived(peer, peer)
-    send_block(8, peer, up)
-    send_block(9, peer, down)
-    send_block(10, peer, mate)
-    piece_arrived(opposite, 0, up)
-    send_piece(11, opposite, 0, peer)
-    piece_arrived(opposite, 1, down)
-    send_piece(12, opposite, 1, peer)
-    send_block(13, opposite, mate)
+    send_block(10, down, mate)
+    send_block(11, peer, mate)
 
     snap_copy.wait()
-    for k in (0, 1, 3, 2):
+    for k in (0, 2, 1, 3):
         block_arrived(block_id(hi, y + k, 1 - core), mate)
 
     def edge_at(ref, half, tile):
@@ -229,48 +213,54 @@
         def _():
             part[k, :, columns(n)] += sums(half_of(k), T, L, columns(n))
 
-    def dest(d):
-        return pl.ds(pl.multiple_of(((z + 8 + d) % 8) * BLOCK, BLOCK), BLOCK)
-
-    def chain_send(k, n, i, d, to):
-        send(
-            part.at[k, dest(d), columns(n)], landed.at[k, n, i], rs_send.at[k, n, i], rs_recv.at[k, n, i], (tm, to)
+    def block_rows(d):
+        return ((z + d) % 8) * BLOCK
+
+    def encode(k, d):
+        first = block_rows(d)
+        powers = []
+        for pair in range(2):
+            rounded = []
+            for q in (2 * pair, 2 * pair + 1):
+                x = part[k, pl.ds(pl.multiple_of(first + q * 8, 8), 8), :]
+                largest = jnp.max(jnp.abs(x), axis=(0, 1), keepdims=True)
+                largest = jnp.broadcast_to(jnp.maximum(largest, 1e-30), (8, 128))
+                power = jnp.ceil(16.0 * jnp.log2(largest)) + 1.0
+                inverse = CODES / jnp.exp2(power * 0.0625)
+                rounded.append(jnp.round(x * jnp.concatenate([inverse] * 4, 1)).astype(jnp.int32))
+                powers.append(power[:4])
+            pair_codes = jnp.concatenate(rounded, 0).astype(jnp.int16)
+            for g in range(4):
+                codes[k, d, pl.ds(g * BLOCK + pair * 16, 16), :] = pair_codes[:, g * 128:(g + 1) * 128]
+        codes[k, d, pl.ds(4 * BLOCK, 16), :] = jnp.concatenate(powers, 0).astype(jnp.int32).astype(jnp.int16)
+
+    def code_copy(k, d):
+        half = half_of(k)
+        slot = jnp.where(lo == half, 0, 8) + d
+        return pltpu.make_async_remote_copy(
+            src_ref=codes.at[k, d], dst_ref=landed.at[slot], send_sem=rs_send.at[k, d], recv_sem=rs_recv.at[slot],
+            device_id=(tm, half * 8 + (z + d) % 8), device_id_type=MESH,
         )
 
-    def chain_add(k, n, i, d, source):
-        arrived(landed.at[k, n, i], rs_recv.at[k, n, i], (tm, source))
-        part[k, dest(d), columns(n)] += landed[k, n, i]
-
-    def reduce_step(k, n, step):
-        if step > 0:
-            chain_add(k, n, step - 1, (4 - step) * way, z_prev)
-        if step < 4:
-            chain_send(k, n, step, (4 - step) * way, z_next)
-            if step > 0:
-                chain_add(k, n, 3 + step, (step - 3) * way, z_next)
-            if step < 3:
-                chain_send(k, n, 4 + step, (step - 3) * way, z_prev)
-            return
-        total[k, n] = part[k, dest(0), columns(n)]
+    def send_codes(k):
+        for d in (4, 3, 5, 2, 6, 1, 7):
+            encode(k, d)
+            code_copy(k, d).start()
 
         @pl.when(lo != half_of(k))
         def _():
-            pltpu.make_async_remote_copy(
-                src_ref=total.at[k, n], dst_ref=other.at[n], send_sem=x_send.at[n], recv_sem=x_recv.at[n],
-                device_id=(tm, x_mate), device_id_type=MESH,
-            ).start()
+            encode(k, 0)
+            code_copy(k, 0).start()
 
     for tile in range(TILES):
         project(0, tile)
-        if tile == 4:
-            for n, b in enumerate((peer_up, peer_down)):
-                block_arrived(b, (up, down)[n])
-                send_block(14 + n, b, mate)
-    for piece in range(2):
-        piece_arrived(peer_opposite, piece, peer)
-    send_block(16, peer_opposite, mate)
-    for n in range(2):
-        window(0, n)
+    for n, b in enumerate((peer_up, peer_down)):
+        block_arrived(b, (up, down)[n])
+        send_block(12 + n, b, mate)
+    window(0, 0)
+    block_arrived(peer_opposite, peer)
+    send_block(14, peer_opposite, mate)
+    window(0, 1)
     for k in (0, 1, 3, 2):
         block_arrived(block_id(1 - hi, y + k, 1 - core), mate)
     project(1, 0)
@@ -278,33 +268,43 @@
     edge_arrived(0)
     for n in range(2):
         window_edge(0, n)
-        reduce_step(0, n, 0)
+    send_codes(0)
     for tile in range(2, TILES):
         project(1, tile)
     for n in range(2):
-        reduce_step(0, n, 1)
+        window(1, n)
     edge_arrived(1)
     for n in range(2):
-        window(1, n)
         window_edge(1, n)
-        reduce_step(1, n, 0)
-        for m in range(2):
-            reduce_step(0, m, 2 + n)
-    for n in range(2):
-        reduce_step(0, n, 4)
-    for step in range(1, 5):
-        for n in range(2):
-            reduce_step(1, n, step)
+    send_codes(1)
 
     mine = jnp.where(lo == hi, 0, 1)
-    for n in range(2):
-        arrived(other.at[n], x_recv.at[n], (tm, x_mate))
-        env = total[mine, n] + other[n]
-        result = out_turn[:, columns(n)] * env + out_cross[:, columns(n)] * swap_parts(env)
-        for q in range(4):
-            for p in range(2):
-                out_ref[q, p, :, columns(n)] = result[q * 8 + p * 4:q * 8 + p * 4 + 4]
-
+    total[...] = part[mine, pl.ds(pl.multiple_of(block_rows(0), BLOCK), BLOCK), :]
+    for slot in (9, 15, 1, 7, 8, 10, 14, 2, 6, 11, 13, 3, 5, 12, 4):
+        pltpu.make_async_remote_copy(
+            src_ref=landed.at[slot], dst_ref=landed.at[slot], send_sem=rs_recv.at[slot], recv_sem=rs_recv.at[slot],
+            device_id=(tm, (rows + 1) % 16), device_id_type=MESH,
+        ).wait_recv()
+        power = landed[slot, pl.ds(4 * BLOCK, 16), :].astype(jnp.int32).astype(jnp.float32)
+        scale = jnp.exp2(power * 0.0625) * (1.0 / CODES)
+        scale = jnp.concatenate([jnp.broadcast_to(scale[4 * q:4 * q + 1], (8, 128)) for q in range(4)], 0)
+        for g in range(4):
+            values = landed[slot, pl.ds(g * BLOCK, BLOCK), :].astype(jnp.int32).astype(jnp.float32)
+            total[:, pl.ds(g * 128, 128)] += values * scale
+    env = total[...]
+    result = out_turn[...] * env + out_cross[...] * swap_parts(env)
+    for q in range(4):
+        for p in range(2):
+            out_ref[q, p] = result[q * 8 + p * 4:q * 8 + p * 4 + 4]
+
+    for k in range(2):
+        for d in range(1, 8):
+            code_copy(k, d).wait_send()
+    code_copy_left = pltpu.make_async_remote_copy(
+        src_ref=codes.at[1 - mine, 0], dst_ref=landed.at[8], send_sem=rs_send.at[1 - mine, 0], recv_sem=rs_recv.at[8],
+        device_id=(tm, (1 - lo) * 8 + z), device_id_type=MESH,
+    )
+    code_copy_left.wait_send()
     for copy in sends:
         copy.wait_send()
 
@@ -317,12 +317,6 @@
                     send_sem=edge_send.at[half, n], recv_sem=edge_recv.at[half, n],
                     device_id=(below, rows), device_id_type=MESH,
                 ).wait_send()
-
-    for n in range(2):
-        pltpu.make_async_remote_copy(
-            src_ref=total.at[1 - mine, n], dst_ref=other.at[n], send_sem=x_send.at[n], recv_sem=x_recv.at[n],
-            device_id=(tm, x_mate), device_id_type=MESH,
-        ).wait_send()
 
 
 def body(snapshots, spod_modes, freq_index, seg_offsets):
@@ -352,15 +346,14 @@
             vmem((BLOCK, S), f32),
             vmem((BLOCK, S), f32),
             vmem((2, HALF, S), f32),
-            vmem((2, 2, 7, BLOCK, 256), f32),
-            vmem((2, 2, BLOCK, 256), f32),
-            vmem((2, BLOCK, 256), f32),
+            vmem((2, 8, 4 * BLOCK + 16, 128), jnp.int16),
+            vmem((16, 4 * BLOCK + 16, 128), jnp.int16),
             vmem((F // 16, 2, M, R), bf16),
+            vmem((BLOCK, S), f32),
             dma, dma,
-            dma((17,)), dma((16, 2)),
+            dma((15,)), dma((16,)),
             dma((2, 2)), dma((2, 2)),
-            dma((2, 2, 7)), dma((2, 2, 7)),
-            dma((2,)), dma((2,)),
+            dma((2, 8)), dma((16,)),
         ],
         compiler_params=pltpu.CompilerParams(
             collective_id=0, has_side_effects=True, vmem_limit_bytes=56 * 1024 * 1024

time: 60.2 us -> 56.1 us (0.932); the launches traced: 59.2 us -> 55.9 us
  Pallas kernels: 57.7 us -> 54.5 us
    pallas_call x1, Pallas kernels: 57.7 us -> 54.5 us  [body(): pl.pallas_call(kernel, out_shape=jax.ShapeDtypeStruct((F // 16, 2, M, S),...]
where the time goes in v4:
time: 56.1 us; the launch traced here: 55.9 us
  Pallas kernels  54.5 us (97%)
  local copies, waits for them, and re-layouts  1.47 us (3%)
    pallas_call x1, Pallas kernels, body(): pl.pallas_call(kernel, out_shape=jax.ShapeDtypeStruct((F // 16, 2, M, S),...  54.5 us
    unnamed x1, local copies, waits for them, and re-layouts  1.47 us

profile of v4, /device:TPU:27, one launch (start us, length us, event | category | flops | bytes accessed | tf_op | source)
XLA Modules:
  0.0 55.9 jit_solution(9871077374316244112)
XLA Ops:
  0.0 54.5 %shard_map.46 = f32[4,2,4,512]{3,2,1,0:T(4,128)} custom-call(s32[64]{0:T(128)} %freq_ref.1, bf16[2048,2048]{1,0:T(8,128)(2,1)} %snap_hbm.1, bf16[4,2,4,2048]{3,2,1,0:T(4,128)(2,1)} %modes_hbm.1, s32[1,512]{1,0:T(1,128)} %bitcast.1), custom_call_target="tpu_custom_call" | custom-call | flops 8000000000 | bytes 10000000 | tf_op jit(solution)/shard_map/pallas_call | solution.py:326
  54.5 1.5 %copy.6 = f32[4,2,4,512]{3,2,1,0:T(4,128)} copy(f32[4,2,4,512]{3,2,1,0:T(4,128)} %shard_map.46) | data formatting | bytes 131072

commit v5 on v4

--- a/solution.py
+++ b/solution.py
@@ -38,10 +38,22 @@
     return jnp.dot(a, b, preferred_element_type=jnp.float32)
 
 
+def to_codes(x):
+    return jnp.round(x).astype(jnp.int32).astype(jnp.int16)
+
+
+def from_codes(codes):
+    return codes.astype(jnp.int32).astype(jnp.float32)
+
+
+def power_above(largest):
+    return jnp.ceil(16.0 * jnp.log2(jnp.maximum(largest, 1e-30))) + 1.0
+
+
 def kernel(
     freq_ref, snap_hbm, modes_hbm, off_ref, out_ref,
     snap, modes, d_high, d_low, w_high, w_low, turn, cross, hann, out_turn, out_cross,
-    part, codes, landed, raw, total,
+    part, codes, landed, raw, total, edge_out, edge_in,
     snap_sem, own_sem, ag_send, ag_recv, edge_send, edge_recv, rs_send, rs_recv,
 ):
     tm = lax.axis_index("tm")
@@ -163,26 +175,40 @@
     for k in (0, 2, 1, 3):
         block_arrived(block_id(hi, y + k, 1 - core), mate)
 
-    def edge_at(ref, half, tile):
-        return ref.at[half, :, pl.ds(tile * L, L)]
+    def edge_copy(half):
+        return pltpu.make_async_remote_copy(
+            src_ref=edge_out.at[half], dst_ref=edge_in.at[half],
+            send_sem=edge_send.at[half], recv_sem=edge_recv.at[half],
+            device_id=(below, rows), device_id_type=MESH,
+        )
+
+    def half_of(k):
+        return hi if k == 0 else 1 - hi
+
+    def to_rows(x):
+        return jnp.broadcast_to(x[:, None, :], (32, 8, 128)).reshape(HALF, 128)
 
     def project(k, tile):
-        half = hi if k == 0 else 1 - hi
+        half = half_of(k)
         p = lax.dot_general(
             modes[half], snap[pl.ds(tile * L, L), :], NT, preferred_element_type=jnp.float32
         )
-        high, low = split(turn[half] * p + cross[half] * swap_parts(p))
+        d = turn[half] * p + cross[half] * swap_parts(p)
+        if tile == 0:
+            largest = jnp.max(jnp.abs(d), axis=1, keepdims=True)
+            largest = jnp.max(jnp.broadcast_to(largest, (HALF, 128)).reshape(32, 8, 128), axis=1)
+            power = power_above(largest)
+            inverse = to_rows(CODES / jnp.exp2(power * 0.0625))
+            edge_out[half, pl.ds(HALF, 32), :] = to_codes(jnp.concatenate([power] * 2, 1))
+            edge_out[half, pl.ds(0, HALF), :] = to_codes(d * jnp.concatenate([inverse] * 2, 1))
+
+            @pl.when(tm > 0)
+            def _():
+                edge_copy(half).start()
+
+        high, low = split(d)
         d_high[half, :, pl.ds(tile * L, L)] = high
         d_low[half, :, pl.ds(tile * L, L)] = low
-        if tile == 0:
-            @pl.when(tm > 0)
-            def _():
-                for n, ref in enumerate((d_high, d_low)):
-                    pltpu.make_async_remote_copy(
-                        src_ref=edge_at(ref, half, 0), dst_ref=edge_at(ref, half, TILES),
-                        send_sem=edge_send.at[half, n], recv_sem=edge_recv.at[half, n],
-                        device_id=(below, rows), device_id_type=MESH,
-                    ).start()
 
     def sums(half, first, length, cols):
         at_t = pl.ds(first, length)
@@ -193,9 +219,6 @@
             + dot(high, w_low[at_t, cols])
         )
 
-    def half_of(k):
-        return hi if k == 0 else 1 - hi
-
     def columns(n):
         return pl.ds(n * 256, 256)
 
@@ -203,10 +226,17 @@
         part[k, :, columns(n)] = sums(half_of(k), 0, T, columns(n))
 
     def edge_arrived(k):
+        half = half_of(k)
+
         @pl.when(tm < 15)
         def _():
-            for n, ref in enumerate((d_high, d_low)):
-                arrived(edge_at(ref, half_of(k), TILES), edge_recv.at[half_of(k), n], (above, rows))
+            arrived(edge_in.at[half], edge_recv.at[half], (above, rows))
+            power = from_codes(edge_in[half, pl.ds(HALF, 32), pl.ds(0, 128)])
+            scale = to_rows(jnp.exp2(power * 0.0625) * (1.0 / CODES))
+            values = from_codes(edge_in[half, pl.ds(0, HALF), :])
+            high, low = split(values * jnp.concatenate([scale] * 2, 1))
+            d_high[half, :, pl.ds(T, L)] = high
+            d_low[half, :, pl.ds(T, L)] = low
 
     def window_edge(k, n):
         @pl.when(tm < 15)
@@ -224,8 +254,7 @@
             for q in (2 * pair, 2 * pair + 1):
                 x = part[k, pl.ds(pl.multiple_of(first + q * 8, 8), 8), :]
                 largest = jnp.max(jnp.abs(x), axis=(0, 1), keepdims=True)
-                largest = jnp.broadcast_to(jnp.maximum(largest, 1e-30), (8, 128))
-                power = jnp.ceil(16.0 * jnp.log2(largest)) + 1.0
+                power = power_above(jnp.broadcast_to(largest, (8, 128)))
                 inverse = CODES / jnp.exp2(power * 0.0625)
                 rounded.append(jnp.round(x * jnp.concatenate([inverse] * 4, 1)).astype(jnp.int32))
                 powers.append(power[:4])
@@ -265,12 +294,17 @@
         block_arrived(block_id(1 - hi, y + k, 1 - core), mate)
     project(1, 0)
     project(1, 1)
-    edge_arrived(0)
-    for n in range(2):
-        window_edge(0, n)
-    send_codes(0)
+
+    def finish_first():
+        edge_arrived(0)
+        for n in range(2):
+            window_edge(0, n)
+        send_codes(0)
+
+    pl.when(tm != 7)(finish_first)
     for tile in range(2, TILES):
         project(1, tile)
+    pl.when(tm == 7)(finish_first)
     for n in range(2):
         window(1, n)
     edge_arrived(1)
@@ -311,12 +345,7 @@
     @pl.when(tm > 0)
     def _():
         for half in range(2):
-            for n, ref in enumerate((d_high, d_low)):
-                pltpu.make_async_remote_copy(
-                    src_ref=edge_at(ref, half, 0), dst_ref=edge_at(ref, half, TILES),
-                    send_sem=edge_send.at[half, n], recv_sem=edge_recv.at[half, n],
-                    device_id=(below, rows), device_id_type=MESH,
-                ).wait_send()
+            edge_copy(half).wait_send()
 
 
 def body(snapshots, spod_modes, freq_index, seg_offsets):
@@ -350,9 +379,11 @@
             vmem((16, 4 * BLOCK + 16, 128), jnp.int16),
             vmem((F // 16, 2, M, R), bf16),
             vmem((BLOCK, S), f32),
+            vmem((2, HALF + 32, L), jnp.int16),
+            vmem((2, HALF + 32, L), jnp.int16),
             dma, dma,
             dma((15,)), dma((16,)),
-            dma((2, 2)), dma((2, 2)),
+            dma((2,)), dma((2,)),
             dma((2, 8)), dma((16,)),
         ],
         compiler_params=pltpu.CompilerParams(

time: 56.1 us -> 50.1 us (0.89)
  Pallas kernels: 54.5 us -> 47.9 us
    pallas_call x1, Pallas kernels: 54.5 us -> 47.9 us  [body(): pl.pallas_call(kernel, out_shape=jax.ShapeDtypeStruct((F // 16, 2, M, S),...]
where the time goes in v5:
time: 50.1 us; the launch traced here: 49.4 us
  Pallas kernels  47.9 us (96%)
  local copies, waits for them, and re-layouts  1.47 us (3%)
    pallas_call x1, Pallas kernels, body(): pl.pallas_call(kernel, out_shape=jax.ShapeDtypeStruct((F // 16, 2, M, S),...  47.9 us
    unnamed x1, local copies, waits for them, and re-layouts  1.47 us

profile of v5, /device:TPU:27, one launch (start us, length us, event | category | flops | bytes accessed | tf_op | source)
XLA Modules:
  0.0 49.4 jit_solution(6001985025665342907)
XLA Ops:
  0.0 47.9 %shard_map.46 = f32[4,2,4,512]{3,2,1,0:T(4,128)} custom-call(s32[64]{0:T(128)} %freq_ref.1, bf16[2048,2048]{1,0:T(8,128)(2,1)} %snap_hbm.1, bf16[4,2,4,2048]{3,2,1,0:T(4,128)(2,1)} %modes_hbm.1, s32[1,512]{1,0:T(1,128)} %bitcast.1), custom_call_target="tpu_custom_call" | custom-call | flops 8000000000 | bytes 10000000 | tf_op jit(solution)/shard_map/pallas_call | solution.py:355
  47.9 1.5 %copy.6 = f32[4,2,4,512]{3,2,1,0:T(4,128)} copy(f32[4,2,4,512]{3,2,1,0:T(4,128)} %shard_map.46) | data formatting | bytes 131072

commit v6 on v5

--- a/solution.py
+++ b/solution.py
@@ -53,13 +53,14 @@
 def kernel(
     freq_ref, snap_hbm, modes_hbm, off_ref, out_ref,
     snap, modes, d_high, d_low, w_high, w_low, turn, cross, hann, out_turn, out_cross,
-    part, codes, landed, raw, total, edge_out, edge_in,
-    snap_sem, own_sem, ag_send, ag_recv, edge_send, edge_recv, rs_send, rs_recv,
+    part, codes, landed, relayed, raw, total, edge_out, edge_in,
+    snap_sem, own_sem, ag_send, ag_recv, edge_send, edge_recv, rs_send, rs_recv, relay_recv,
 ):
     tm = lax.axis_index("tm")
     rows = lax.axis_index("rows")
     hi, y, core = tm // 8, (tm // 2) % 4, tm % 2
     lo, z = rows // 8, rows % 8
+    way = 1 - 2 * core
 
     def block_id(h, yy, c):
         return h * 8 + (yy % 4) * 2 + c
@@ -82,8 +83,10 @@
     barrier = pltpu.get_barrier_semaphore()
     for b in (mate, cross_edge, up, down, opposite, peer):
         pl.semaphore_signal(barrier, inc=1, device_id=(b, rows), device_id_type=MESH)
-    for d in range(1, 16):
-        pl.semaphore_signal(barrier, inc=1, device_id=(tm, (rows + d) % 16), device_id_type=MESH)
+    for d in (1, 2, 6, 7):
+        pl.semaphore_signal(barrier, inc=1, device_id=(tm, lo * 8 + (z + d) % 8), device_id_type=MESH)
+    for d in (0, 1, 2, 6, 7):
+        pl.semaphore_signal(barrier, inc=1, device_id=(tm, (1 - lo) * 8 + (z + d) % 8), device_id_type=MESH)
 
     lane = lax.broadcasted_iota(jnp.int32, (8, L), 1)
     upper = lax.broadcasted_iota(jnp.int32, (8, L), 0) < 4
@@ -132,7 +135,7 @@
         pair = [raw[2 * n + q].astype(jnp.float32).reshape(8, R) for q in range(2)]
         own[pl.ds(n * 16, 16), :] = jnp.concatenate(pair, 0).astype(jnp.bfloat16)
 
-    pl.semaphore_wait(barrier, 21)
+    pl.semaphore_wait(barrier, 15)
 
     sends = []
 
@@ -243,43 +246,68 @@
         def _():
             part[k, :, columns(n)] += sums(half_of(k), T, L, columns(n))
 
-    def block_rows(d):
-        return ((z + d) % 8) * BLOCK
-
-    def encode(k, d):
-        first = block_rows(d)
+    block_of = (4, 3, -3, 1, -1, 2, -2, 0)
+    relay_of = (2, 1, -1)
+
+    def along(d):
+        return (z + 8 + d * way) % 8
+
+    def block(d):
+        return pl.ds(pl.multiple_of(along(d) * BLOCK, BLOCK), BLOCK)
+
+    def encode(k, i):
+        first = along(block_of[i]) * BLOCK
         powers = []
         for pair in range(2):
-            rounded = []
+            scaled = []
             for q in (2 * pair, 2 * pair + 1):
                 x = part[k, pl.ds(pl.multiple_of(first + q * 8, 8), 8), :]
                 largest = jnp.max(jnp.abs(x), axis=(0, 1), keepdims=True)
                 power = power_above(jnp.broadcast_to(largest, (8, 128)))
                 inverse = CODES / jnp.exp2(power * 0.0625)
-                rounded.append(jnp.round(x * jnp.concatenate([inverse] * 4, 1)).astype(jnp.int32))
+                scaled.append(x * jnp.concatenate([inverse] * 4, 1))
                 powers.append(power[:4])
-            pair_codes = jnp.concatenate(rounded, 0).astype(jnp.int16)
+            pair_codes = to_codes(jnp.concatenate(scaled, 0))
             for g in range(4):
-                codes[k, d, pl.ds(g * BLOCK + pair * 16, 16), :] = pair_codes[:, g * 128:(g + 1) * 128]
-        codes[k, d, pl.ds(4 * BLOCK, 16), :] = jnp.concatenate(powers, 0).astype(jnp.int32).astype(jnp.int16)
-
-    def code_copy(k, d):
+                codes[k, i, pl.ds(g * BLOCK + pair * 16, 16), :] = pair_codes[:, g * 128:(g + 1) * 128]
+        codes[k, i, pl.ds(4 * BLOCK, 16), :] = to_codes(jnp.concatenate(powers, 0))
+
+    def decode(ref):
+        scale = jnp.exp2(from_codes(ref[pl.ds(4 * BLOCK, 16), :]) * 0.0625) * (1.0 / CODES)
+        scale = jnp.concatenate([jnp.broadcast_to(scale[4 * q:4 * q + 1], (8, 128)) for q in range(4)], 0)
+        return jnp.concatenate([from_codes(ref[pl.ds(g * BLOCK, BLOCK), :]) * scale for g in range(4)], 1)
+
+    def code_copy(k, i):
         half = half_of(k)
-        slot = jnp.where(lo == half, 0, 8) + d
+        if i < 3:
+            dst, recv_sem = relayed.at[k, i], relay_recv.at[k, i]
+            owner = lo * 8 + along(relay_of[i])
+        else:
+            slot = jnp.where(lo == half, 0, 5) + i - 3
+            dst, recv_sem = landed.at[slot], rs_recv.at[slot]
+            owner = half * 8 + along(block_of[i])
         return pltpu.make_async_remote_copy(
-            src_ref=codes.at[k, d], dst_ref=landed.at[slot], send_sem=rs_send.at[k, d], recv_sem=rs_recv.at[slot],
-            device_id=(tm, half * 8 + (z + d) % 8), device_id_type=MESH,
+            src_ref=codes.at[k, i], dst_ref=dst, send_sem=rs_send.at[k, i], recv_sem=recv_sem,
+            device_id=(tm, owner), device_id_type=MESH,
         )
 
     def send_codes(k):
-        for d in (4, 3, 5, 2, 6, 1, 7):
-            encode(k, d)
-            code_copy(k, d).start()
+        for i in range(5):
+            encode(k, i)
+            code_copy(k, i).start()
 
         @pl.when(lo != half_of(k))
         def _():
-            encode(k, 0)
-            code_copy(k, 0).start()
+            encode(k, 7)
+            code_copy(k, 7).start()
+
+    def relay(k):
+        for i, sources in ((5, (1, 0)), (6, (2,))):
+            for n in sources:
+                arrived(relayed.at[k, n], relay_recv.at[k, n], (tm, lo * 8 + along(-relay_of[n])))
+                part[k, block(block_of[i]), :] += decode(relayed.at[k, n])
+            encode(k, i)
+            code_copy(k, i).start()
 
     for tile in range(TILES):
         project(0, tile)
@@ -311,20 +339,14 @@
     for n in range(2):
         window_edge(1, n)
     send_codes(1)
+    relay(0)
+    relay(1)
 
     mine = jnp.where(lo == hi, 0, 1)
-    total[...] = part[mine, pl.ds(pl.multiple_of(block_rows(0), BLOCK), BLOCK), :]
-    for slot in (9, 15, 1, 7, 8, 10, 14, 2, 6, 11, 13, 3, 5, 12, 4):
-        pltpu.make_async_remote_copy(
-            src_ref=landed.at[slot], dst_ref=landed.at[slot], send_sem=rs_recv.at[slot], recv_sem=rs_recv.at[slot],
-            device_id=(tm, (rows + 1) % 16), device_id_type=MESH,
-        ).wait_recv()
-        power = landed[slot, pl.ds(4 * BLOCK, 16), :].astype(jnp.int32).astype(jnp.float32)
-        scale = jnp.exp2(power * 0.0625) * (1.0 / CODES)
-        scale = jnp.concatenate([jnp.broadcast_to(scale[4 * q:4 * q + 1], (8, 128)) for q in range(4)], 0)
-        for g in range(4):
-            values = landed[slot, pl.ds(g * BLOCK, BLOCK), :].astype(jnp.int32).astype(jnp.float32)
-            total[:, pl.ds(g * 128, 128)] += values * scale
+    total[...] = part[mine, block(0), :]
+    for slot in (9, 0, 1, 5, 6, 2, 3, 7, 8):
+        arrived(landed.at[slot], rs_recv.at[slot], (tm, lo * 8 + along(1)))
+        total[...] += decode(landed.at[slot])
     env = total[...]
     result = out_turn[...] * env + out_cross[...] * swap_parts(env)
     for q in range(4):
@@ -332,13 +354,12 @@
             out_ref[q, p] = result[q * 8 + p * 4:q * 8 + p * 4 + 4]
 
     for k in range(2):
-        for d in range(1, 8):
-            code_copy(k, d).wait_send()
-    code_copy_left = pltpu.make_async_remote_copy(
-        src_ref=codes.at[1 - mine, 0], dst_ref=landed.at[8], send_sem=rs_send.at[1 - mine, 0], recv_sem=rs_recv.at[8],
+        for i in range(7):
+            code_copy(k, i).wait_send()
+    pltpu.make_async_remote_copy(
+        src_ref=codes.at[1 - mine, 7], dst_ref=landed.at[9], send_sem=rs_send.at[1 - mine, 7], recv_sem=rs_recv.at[9],
         device_id=(tm, (1 - lo) * 8 + z), device_id_type=MESH,
-    )
-    code_copy_left.wait_send()
+    ).wait_send()
     for copy in sends:
         copy.wait_send()
 
@@ -354,7 +375,7 @@
     dma = pltpu.SemaphoreType.DMA
     return pl.pallas_call(
         kernel,
-        out_shape=jax.ShapeDtypeStruct((F // 16, 2, M, S), f32),
+        out_shape=vmem((F // 16, 2, M, S), f32),
         in_specs=[
             pl.BlockSpec(memory_space=pltpu.SMEM),
             pl.BlockSpec(memory_space=pl.ANY),
@@ -376,7 +397,8 @@
             vmem((BLOCK, S), f32),
             vmem((2, HALF, S), f32),
             vmem((2, 8, 4 * BLOCK + 16, 128), jnp.int16),
-            vmem((16, 4 * BLOCK + 16, 128), jnp.int16),
+            vmem((10, 4 * BLOCK + 16, 128), jnp.int16),
+            vmem((2, 3, 4 * BLOCK + 16, 128), jnp.int16),
             vmem((F // 16, 2, M, R), bf16),
             vmem((BLOCK, S), f32),
             vmem((2, HALF + 32, L), jnp.int16),
@@ -384,7 +406,7 @@
             dma, dma,
             dma((15,)), dma((16,)),
             dma((2,)), dma((2,)),
-            dma((2, 8)), dma((16,)),
+            dma((2, 8)), dma((10,)), dma((2, 3)),
         ],
         compiler_params=pltpu.CompilerParams(
             collective_id=0, has_side_effects=True, vmem_limit_bytes=56 * 1024 * 1024

time: 50.1 us -> 47 us (0.938)
  Pallas kernels: 47.9 us -> 45.9 us
  local copies, waits for them, and re-layouts: 1.47 us -> 0.63 us
    pallas_call x1, Pallas kernels: 47.9 us -> 45.9 us  [body(): pl.pallas_call(kernel, out_shape=vmem((F // 16, 2, M, S), f32), in_specs=...]
    unnamed x1, local copies, waits for them, and re-layouts: 1.47 us -> 0.63 us
where the time goes in v6:
time: 47 us; the launch traced here: 46.6 us
  Pallas kernels  45.9 us (98%)
  local copies, waits for them, and re-layouts  0.63 us (1%)
    pallas_call x1, Pallas kernels, body(): pl.pallas_call(kernel, out_shape=vmem((F // 16, 2, M, S), f32), in_specs=...  45.9 us

profile of v6, /device:TPU:27, one launch (start us, length us, event | category | flops | bytes accessed | tf_op | source)
XLA Modules:
  0.0 46.6 jit_solution(16858884903269682829)
XLA Ops:
  0.0 45.9 %shard_map.46 = f32[4,2,4,512]{3,2,1,0:T(4,128)S(1)} custom-call(s32[64]{0:T(128)} %freq_ref.1, bf16[2048,2048]{1,0:T(8,128)(2,1)} %snap_hbm.1, bf16[4,2,4,2048]{3,2,1,0:T(4,128)(2,1)} %modes_hbm.1, s32[1,512]{1,0:T(1,128)} %bitcast.1), custom_call_target="tpu_custom_call" | custom-call | flops 8000000000 | bytes 10000000 | tf_op jit(solution)/shard_map/pallas_call | solution.py:376
  45.9 0.6 %copy.6 = f32[4,2,4,512]{3,2,1,0:T(4,128)} copy(f32[4,2,4,512]{3,2,1,0:T(4,128)S(1)} %shard_map.46) | data formatting | bytes 131072

commit v7 on v6

--- a/solution.py
+++ b/solution.py
@@ -292,9 +292,11 @@
         )
 
     def send_codes(k):
-        for i in range(5):
-            encode(k, i)
-            code_copy(k, i).start()
+        for group in ((0, 1, 2), (3, 4)):
+            for i in group:
+                encode(k, i)
+            for i in group:
+                code_copy(k, i).start()
 
         @pl.when(lo != half_of(k))
         def _():
@@ -311,12 +313,13 @@
 
     for tile in range(TILES):
         project(0, tile)
-    for n, b in enumerate((peer_up, peer_down)):
-        block_arrived(b, (up, down)[n])
-        send_block(12 + n, b, mate)
-    window(0, 0)
+        if tile == 4:
+            for n, b in enumerate((peer_up, peer_down)):
+                block_arrived(b, (up, down)[n])
+                send_block(12 + n, b, mate)
     block_arrived(peer_opposite, peer)
     send_block(14, peer_opposite, mate)
+    window(0, 0)
     window(0, 1)
     for k in (0, 1, 3, 2):
         block_arrived(block_id(1 - hi, y + k, 1 - core), mate)

time: 47 us -> 44.6 us (0.949)
  Pallas kernels: 45.9 us -> 43.8 us
    pallas_call x1, Pallas kernels: 45.9 us -> 43.8 us  [body(): pl.pallas_call(kernel, out_shape=vmem((F // 16, 2, M, S), f32), in_specs=...]
where the time goes in v7:
time: 44.6 us; the launch traced here: 44.5 us
  Pallas kernels  43.8 us (98%)
  local copies, waits for them, and re-layouts  0.63 us (1%)
    pallas_call x1, Pallas kernels, body(): pl.pallas_call(kernel, out_shape=vmem((F // 16, 2, M, S), f32), in_specs=...  43.8 us

profile of v7, /device:TPU:27, one launch (start us, length us, event | category | flops | bytes accessed | tf_op | source)
XLA Modules:
  0.0 44.5 jit_solution(466845284713963640)
XLA Ops:
  0.0 43.8 %shard_map.46 = f32[4,2,4,512]{3,2,1,0:T(4,128)S(1)} custom-call(s32[64]{0:T(128)} %freq_ref.1, bf16[2048,2048]{1,0:T(8,128)(2,1)} %snap_hbm.1, bf16[4,2,4,2048]{3,2,1,0:T(4,128)(2,1)} %modes_hbm.1, s32[1,512]{1,0:T(1,128)} %bitcast.1), custom_call_target="tpu_custom_call" | custom-call | flops 8000000000 | bytes 10000000 | tf_op jit(solution)/shard_map/pallas_call | solution.py:379
  43.8 0.6 %copy.6 = f32[4,2,4,512]{3,2,1,0:T(4,128)} copy(f32[4,2,4,512]{3,2,1,0:T(4,128)S(1)} %shard_map.46) | data formatting | bytes 131072

commit v8 on v7

--- a/solution.py
+++ b/solution.py
@@ -162,11 +162,11 @@
     send_block(2, tm, up)
     send_block(3, tm, down)
     send_block(4, tm, mate)
-    block_arrived(opposite, opposite)
-    send_block(5, opposite, peer)
     block_arrived(peer, peer)
     send_block(6, peer, up)
     send_block(7, peer, down)
+    block_arrived(opposite, opposite)
+    send_block(5, opposite, peer)
     send_block(8, opposite, mate)
     block_arrived(up, up)
     send_block(9, up, mate)
@@ -304,7 +304,7 @@
             code_copy(k, 7).start()
 
     def relay(k):
-        for i, sources in ((5, (1, 0)), (6, (2,))):
+        for i, sources in ((6, (2,)), (5, (1, 0))):
             for n in sources:
                 arrived(relayed.at[k, n], relay_recv.at[k, n], (tm, lo * 8 + along(-relay_of[n])))
                 part[k, block(block_of[i]), :] += decode(relayed.at[k, n])

time: 44.6 us -> 44.7 us (level)
  no operation moved by 1% of the time
where the time goes in v8:
time: 44.7 us; the launch traced here: 44.6 us
  Pallas kernels  44 us (98%)
  local copies, waits for them, and re-layouts  0.63 us (1%)
    pallas_call x1, Pallas kernels, body(): pl.pallas_call(kernel, out_shape=vmem((F // 16, 2, M, S), f32), in_specs=...  44 us

profile of v8, /device:TPU:27, one launch (start us, length us, event | category | flops | bytes accessed | tf_op | source)
XLA Modules:
  0.0 44.6 jit_solution(16283225977208059693)
XLA Ops:
  0.0 44.0 %shard_map.46 = f32[4,2,4,512]{3,2,1,0:T(4,128)S(1)} custom-call(s32[64]{0:T(128)} %freq_ref.1, bf16[2048,2048]{1,0:T(8,128)(2,1)} %snap_hbm.1, bf16[4,2,4,2048]{3,2,1,0:T(4,128)(2,1)} %modes_hbm.1, s32[1,512]{1,0:T(1,128)} %bitcast.1), custom_call_target="tpu_custom_call" | custom-call | flops 8000000000 | bytes 10000000 | tf_op jit(solution)/shard_map/pallas_call | solution.py:379
  44.0 0.6 %copy.6 = f32[4,2,4,512]{3,2,1,0:T(4,128)} copy(f32[4,2,4,512]{3,2,1,0:T(4,128)S(1)} %shard_map.46) | data formatting | bytes 131072
